TPU v7x, 32 devices: a whole 2x2x4 slice. The times are simulated.
32 devices in a mesh: group: 4 (over y, x), local: 8 (over z, core).
Axes of the slice: x: 2, y: 2, z: 4, core: 2. Of those that a mesh axis runs over, the one named last changes fastest.
Arguments:
- features: bfloat16 [192, 7168], P(('group', 'local')), may hold values from -6 to 6
- cotangent: bfloat16 [192, 7168], P(('group', 'local')), may hold values from -6 to 6
- expert_ids: int32 [192, 4], P(('group', 'local')), may hold values from 0 to 7, as said below
- gates: float32 [192, 4], P(('group', 'local')), may hold values from 0.1 to 1
- w_gate: bfloat16 [8, 7168, 2048], P('local', None, 'group'), may hold values from -0.0625 to 0.0625
- w_up: bfloat16 [8, 7168, 2048], P('local', None, 'group'), may hold values from -0.0625 to 0.0625
- w_down: bfloat16 [8, 2048, 7168], P('local', 'group'), may hold values from -0.125 to 0.125
Outputs:
- grad_features: float32 [192, 7168], P(('group', 'local'))
- grad_gate: bfloat16 [8, 7168, 2048], P('local', None, 'group')
- grad_up: bfloat16 [8, 7168, 2048], P('local', None, 'group')
- grad_down: bfloat16 [8, 2048, 7168], P('local', 'group')
Inputs may be any that keep to these rules, and one draw needn't show every extreme that they name: `expert_ids`: each row names 4 different experts, all of them in at most 3 expert groups, expert e lying in group e // 2.
All inputs are finite; a program needn't handle non-finite values.
Results may differ from a plain program's by a relative error of at most 0.013.
Values may be sent and summed in bfloat16 or wider, within the bound.
A program may use at most 192 MiB of HBM per device.

v0:
```python
import jax
import jax.numpy as jnp
from jax import lax
from jax.sharding import PartitionSpec as P

BOTH = ("group", "local")


def silu_parts(pre):
    sig = jax.nn.sigmoid(pre)
    return (pre * sig, sig * (1.0 + pre * (1.0 - sig)))


def body(features, cotangent, expert_ids, gates, w_gate, w_up, w_down):
    experts = lax.axis_size("local")
    devices = experts * lax.axis_size("group")
    tok_rows, width = features.shape
    rows = devices * tok_rows
    hits = expert_ids[..., None] == jnp.arange(experts, dtype=jnp.int32)
    on = jnp.sum(hits.astype(jnp.float32), axis=1)
    weight = jnp.sum(jnp.where(hits, gates[..., None], 0.0), axis=1)
    routes = lax.all_gather(jnp.concatenate([on, weight], axis=1)[None], BOTH, axis=0, tiled=True)
    all_x = lax.all_gather(features[None], BOTH, axis=0, tiled=True)
    all_g = lax.all_gather(cotangent[None], BOTH, axis=0, tiled=True)
    me = lax.axis_index("local")
    routes = routes.reshape(rows, 2 * experts)
    on = lax.dynamic_slice_in_dim(routes, me, 1, axis=1)
    weight = lax.dynamic_slice_in_dim(routes, me + experts, 1, axis=1)
    rows_x = jnp.where(on > 0.0, all_x.reshape(rows, width), jnp.bfloat16(0))
    rows_g = (weight * all_g.reshape(rows, width).astype(jnp.float32)).astype(jnp.bfloat16)
    gate_w = w_gate[0]
    up_w = w_up[0]
    down_w = w_down[0]
    pre_gate = jnp.dot(rows_x, gate_w, preferred_element_type=jnp.float32)
    pre_up = jnp.dot(rows_x, up_w, preferred_element_type=jnp.float32)
    act, slope = silu_parts(pre_gate)
    hidden = (act * pre_up).astype(jnp.bfloat16)
    d_hidden = jnp.dot(rows_g, down_w.T, preferred_element_type=jnp.float32)
    d_gate = (d_hidden * pre_up * slope).astype(jnp.bfloat16)
    d_up = (d_hidden * act).astype(jnp.bfloat16)
    part = jnp.dot(d_gate, gate_w.T, preferred_element_type=jnp.float32)
    part = part + jnp.dot(d_up, up_w.T, preferred_element_type=jnp.float32)
    part = lax.optimization_barrier(part.astype(jnp.bfloat16))
    summed = lax.psum_scatter(
        part.reshape(devices, tok_rows, width), BOTH, scatter_dimension=0, tiled=True
    )
    grad_down = jnp.dot(hidden.T, rows_g, preferred_element_type=jnp.float32).astype(jnp.bfloat16)
    grad_gate = jnp.dot(rows_x.T, d_gate, preferred_element_type=jnp.float32).astype(jnp.bfloat16)
    grad_up = jnp.dot(rows_x.T, d_up, preferred_element_type=jnp.float32).astype(jnp.bfloat16)
    return (summed[0].astype(jnp.float32), grad_gate[None], grad_up[None], grad_down[None])


def solution(mesh):
    tokens = P(BOTH, None)
    wide = P("local", None, "group")
    tall = P("local", "group", None)
    return jax.shard_map(
        body,
        mesh=mesh,
        in_specs=(tokens, tokens, tokens, tokens, wide, wide, tall),
        out_specs=(tokens, wide, wide, tall),
        check_vma=False,
    )
```

profile of v0, /device:TPU:0, one launch (start us, length us, event | category | flops | bytes accessed | tf_op | source)
XLA Modules:
  0.0 309.0 jit_solution(17703085022566899046)
XLA Ops:
  7.2 0.7 all-gather.11.cloned.1.call-update
  7.9 0.7 all-gather.9.cloned.1.call-update
  8.7 0.8 copy.17
  9.5 0.8 copy.18
  10.4 44.0 %all-gather.3 = f32[32,6,16]{2,1,0:T(8,128)S(1)} all-gather(f32[1,6,16]{2,1,0:T(8,128)S(1)} %maximum_bitcast_fusion), channel_id=2, replica_groups=mesh['group'=4,'local'=8] {'group','local'}, dimensions={0}, use_global_device_ids=true | all-gather | bytes 12672 | tf_op jit(solution)/shard_map/all_gather | solution.py:22
  55.5 18.8 %all-gather.11.cloned.1.call-done = bf16[32,6,7168]{2,1,0:T(8,128)(2,1)} async-done(((bf16[1,6,7168]{2,1,0:T(8,128)(2,1)}), bf16[32,6,7168]{2,1,0:T(8,128)(2,1)}) %all-gather.11.cloned.1.call-update) | async-done | bytes 2752528 | tf_op jit(solution)/shard_map/all_gather | solution.py:23
  74.3 4.3 %broadcast_select_fusion = bf16[32,6,7168]{2,1,0:T(8,128)(2,1)} fusion(bf16[32,6,7168]{2,1,0:T(8,128)(2,1)} %all-gather.11.cloned.1.call-done, pred[32,6]{1,0:T(8,128)(4,1)S(1)} %broadcast_in_dim.57), kind=kLoop, calls=%fused_computation.19 | loop fusion | flops 1376256 | bytes 5505216 | tf_op jit(solution)/shard_map/jit(_where)/select_n | solution.py:29
  78.5 4.8 %select_n.24 = bf16[192,7168]{1,0:T(8,128)(2,1)} reshape(bf16[32,6,7168]{2,1,0:T(8,128)(2,1)} %broadcast_select_fusion) | data formatting | bytes 5505024 | tf_op jit(solution)/shard_map/jit(_where)/select_n | solution.py:29
  83.3 5.7 %fusion.6 = f32[192,512]{1,0:T(8,128)S(1)} fusion(bf16[192,7168]{1,0:T(8,128)(2,1)} %select_n.24, bf16[1,7168,512]{2,1,0:T(8,128)(2,1)} %param.11), kind=kOutput, calls=%fused_computation.10 | convolution fusion | flops 1409286144 | bytes 10485760 | tf_op jit(solution)/shard_map/dot_general | solution.py:34
  89.4 2.4 fusion.9
  91.8 44.8 %all-gather.9.cloned.1.call-done = bf16[32,6,7168]{2,1,0:T(8,128)(2,1)} async-done(((bf16[1,6,7168]{2,1,0:T(8,128)(2,1)}), bf16[32,6,7168]{2,1,0:T(8,128)(2,1)}) %all-gather.9.cloned.1.call-update) | async-done | bytes 2752528 | tf_op jit(solution)/shard_map/all_gather | solution.py:24
  136.6 4.8 %multiply_convert_fusion = bf16[32,6,7168]{2,1,0:T(8,128)(2,1)} fusion(f32[32,6]{1,0:T(8,128)S(1)} %mul.38, bf16[32,6,7168]{2,1,0:T(8,128)(2,1)} %all-gather.9.cloned.1.call-done), kind=kLoop, calls=%fused_computation.17 | loop fusion | flops 4128768 | bytes 5505792 | tf_op jit(solution)/shard_map/convert_element_type | solution.py:30
  141.3 4.8 %convert_element_type.50 = bf16[192,7168]{1,0:T(8,128)(2,1)} reshape(bf16[32,6,7168]{2,1,0:T(8,128)(2,1)} %multiply_convert_fusion) | data formatting | bytes 5505024 | tf_op jit(solution)/shard_map/convert_element_type | solution.py:30
  146.1 6.6 %multiply_convert_fusion.4 = (bf16[192,512]{1,0:T(8,128)(2,1)S(1)}, bf16[192,512]{1,0:T(8,128)(2,1)S(1)}) fusion(f32[192,512]{1,0:T(8,128)S(1)} %fusion.6, f32[192,512]{1,0:T(8,128)} %fusion.9, bf16[192,7168]{1,0:T(8,128)(2,1)} %convert_element_type.50, bf16[1,512,7168]{2,1,0:T(8,128)(2,1)} %param.13), kind=kOutput, calls=%fused_computation.23 | convolution fusion | flops 1410564096 | bytes 11272192 | tf_op jit(solution)/shard_map/dot_general | solution.py:38
  152.8 2.5 fusion.4
  155.4 2.5 fusion.3
  157.9 2.7 reshape.43
  160.7 3.2 %reshape.62 = bf16[192,7168]{1,0:T(8,128)(2,1)S(1)} reshape(bf16[32,6,7168]{2,1,0:T(8,128)(2,1)} %all-gather.11.cloned.1.call-done) | data formatting | bytes 5505024
  164.0 5.2 %reshape.63 = f32[192,7168]{1,0:T(8,128)} reshape(bf16[32,6,7168]{2,1,0:T(8,128)(2,1)} %all-gather.9.cloned.1.call-done) | data formatting | bytes 8257536 | tf_op jit(solution)/shard_map/convert_element_type | solution.py:30
  169.2 5.3 %fusion.1 = bf16[1,7168,512]{2,1,0:T(8,128)(2,1)} fusion(bf16[192,512]{1,0:T(8,128)(2,1)S(1)} %copy-done.3, bf16[192,7168]{1,0:T(8,128)(2,1)S(1)} %reshape.62, pred[192]{0:T(512)(128)(4,1)S(1)} %copy-done.9), kind=kOutput, calls=%fused_computation.4 | convolution fusion | flops 1414332416 | bytes 10289344 | tf_op jit(solution)/shard_map/dot_general | solution.py:49
  174.5 5.3 %fusion = bf16[1,7168,512]{2,1,0:T(8,128)(2,1)} fusion(bf16[192,512]{1,0:T(8,128)(2,1)S(1)} %copy-done.5, bf16[192,7168]{1,0:T(8,128)(2,1)S(1)} %reshape.62, pred[192]{0:T(512)(128)(4,1)S(1)} %copy-done.9), kind=kOutput, calls=%fused_computation.3 | convolution fusion | flops 1414332416 | bytes 10289344 | tf_op jit(solution)/shard_map/dot_general | solution.py:48
  179.8 5.2 %fusion.2 = bf16[1,512,7168]{2,1,0:T(8,128)(2,1)} fusion(f32[192,7168]{1,0:T(8,128)S(1)} %bitcast.36, f32[192]{0:T(256)S(1)} %copy-done.7, f32[192,512]{1,0:T(8,128)S(1)} %copy-done.1, f32[192,512]{1,0:T(8,128)S(1)} %fusion.6), kind=kOutput, calls=%fused_computation.5 | convolution fusion | flops 1416298496 | bytes 13632256 | tf_op jit(solution)/shard_map/dot_general | solution.py:47
  185.1 115.8 %reduce-scatter.2.cloned.1.call-done = bf16[1,6,7168]{2,1,0:T(8,128)(2,1)} async-done(((bf16[32,6,7168]{2,1,0:T(8,128)(2,1)}), bf16[1,6,7168]{2,1,0:T(8,128)(2,1)}) %reduce-scatter.2.cloned.1.call-update) | async-done | bytes 86032 | tf_op jit(solution)/shard_map/reduce_scatter | solution.py:44
  300.8 1.6 bitcast_convert_fusion
  (51 shorter events, 1.7 us)
Async XLA Ops:
  7.2 67.1 %all-gather.11.cloned.1.call-start = ((), (), s32[]{:S(2)}) async-start(), calls=%async_computation.3 | async-start | bytes 3784704 | tf_op jit(solution)/shard_map/all_gather | solution.py:23
  7.9 128.7 %all-gather.9.cloned.1.call-start = ((), (), s32[]{:S(2)}) async-start(), calls=%async_computation.2 | async-start | bytes 3784704 | tf_op jit(solution)/shard_map/all_gather | solution.py:24
  8.6 292.2 %reduce-scatter.2.cloned.1.call-start = ((), (), s32[]{:S(2)}) async-start(), calls=%async_computation.1 | async-start | bytes 3784704 | tf_op jit(solution)/shard_map/reduce_scatter | solution.py:44
  54.6 0.5 copy-start.8
  55.3 18.9 %copy-start.6 = (f32[192]{0:T(256)}, f32[192]{0:T(256)S(1)}, u32[]{:S(2)}) copy-start(f32[192]{0:T(256)S(1)} %dynamic-slice_reduce_fusion) | copy-start | bytes 2308
  78.5 10.5 %slice-start.4 = ((s8[7340032]{0:T(1024)(128)(4,1)}), s8[3145728]{0:T(1024)(128)(4,1)S(1)}, s32[]{:S(2)}) async-start(s8[7340032]{0:T(1024)(128)(4,1)} %bitcast.39), calls=%async_computation.8 | async-start | bytes 6291456
  83.3 5.7 %slice-start.5 = ((s8[7340032]{0:T(1024)(128)(4,1)}), s8[4194304]{0:T(1024)(128)(4,1)S(1)}, s32[]{:S(2)}) async-start(s8[7340032]{0:T(1024)(128)(4,1)} %bitcast.39), calls=%async_computation.9 | async-start | bytes 8388608
  83.3 6.1 %copy-start = (bf16[192,7168]{1,0:T(8,128)(2,1)S(1)}, bf16[192,7168]{1,0:T(8,128)(2,1)}, u32[]{:S(2)}) copy-start(bf16[192,7168]{1,0:T(8,128)(2,1)} %select_n.24) | copy-start | bytes 8257540
  141.3 11.5 %slice-start.2 = ((s8[7340032]{0:T(1024)(128)(4,1)}), s8[3145728]{0:T(1024)(128)(4,1)S(1)}, s32[]{:S(2)}) async-start(s8[7340032]{0:T(1024)(128)(4,1)} %bitcast.37), calls=%async_computation.6 | async-start | bytes 6291456
  146.1 6.7 %slice-start.3 = ((s8[7340032]{0:T(1024)(128)(4,1)}), s8[4194304]{0:T(1024)(128)(4,1)S(1)}, s32[]{:S(2)}) async-start(s8[7340032]{0:T(1024)(128)(4,1)} %bitcast.37), calls=%async_computation.7 | async-start | bytes 8388608
  146.1 9.3 %slice-start.6 = ((s8[7340032]{0:T(1024)(128)(4,1)}), s8[4194304]{0:T(1024)(128)(4,1)S(1)}, s32[]{:S(2)}) async-start(s8[7340032]{0:T(1024)(128)(4,1)} %bitcast.41), calls=%async_computation.10 | async-start | bytes 8388608
  152.8 2.6 copy-start.4
  152.8 2.6 copy-start.2
  152.8 2.6 slice-start.7
  163.9 5.2 %copy-start.3 = (bf16[192,512]{1,0:T(8,128)(2,1)S(1)}, bf16[192,512]{1,0:T(8,128)(2,1)}, u32[]{:S(2)}) copy-start(bf16[192,512]{1,0:T(8,128)(2,1)} %copy-done.2) | copy-start | bytes 589828
  164.0 5.2 %copy-start.9 = (pred[192]{0:T(512)(128)(4,1)S(1)}, pred[192]{0:T(512)(128)(4,1)}, u32[]{:S(2)}) copy-start(pred[192]{0:T(512)(128)(4,1)} %copy-done.8) | copy-start | bytes 580
  169.2 5.3 %copy-start.5 = (bf16[192,512]{1,0:T(8,128)(2,1)S(1)}, bf16[192,512]{1,0:T(8,128)(2,1)}, u32[]{:S(2)}) copy-start(bf16[192,512]{1,0:T(8,128)(2,1)} %copy-done.4) | copy-start | bytes 589828
  169.2 10.6 %slice-start = ((s8[5505024]{0:T(1024)(128)(4,1)}), s8[4194304]{0:T(1024)(128)(4,1)S(1)}, s32[]{:S(2)}) async-start(s8[5505024]{0:T(1024)(128)(4,1)} %bitcast.35), calls=%async_computation.4 | async-start | bytes 8388608
  174.5 5.3 %slice-start.1 = ((s8[5505024]{0:T(1024)(128)(4,1)}), s8[1310720]{0:T(1024)(128)(4,1)S(1)}, s32[]{:S(2)}) async-start(s8[5505024]{0:T(1024)(128)(4,1)} %bitcast.35), calls=%async_computation.5 | async-start | bytes 2621440
  174.5 5.3 %copy-start.1 = (f32[192,512]{1,0:T(8,128)S(1)}, f32[192,512]{1,0:T(8,128)}, u32[]{:S(2)}) copy-start(f32[192,512]{1,0:T(8,128)} %fusion.9) | copy-start | bytes 1179652
  174.5 5.3 %copy-start.7 = (f32[192]{0:T(256)S(1)}, f32[192]{0:T(256)}, u32[]{:S(2)}) copy-start(f32[192]{0:T(256)} %copy-done.6) | copy-start | bytes 2308
Sparse Core Ops, SparseCore 0:
  10.8 63.3 all-gather.10
  77.1 59.4 all-gather.8
  160.8 139.9 reduce-scatter.1
where the time goes:
time: 309 us
  waiting for transfers between devices  181 us (59%)
  blocking collectives  44 us (14%)
  matrix products  35.6 us (12%)
  local copies, waits for them, and re-layouts  23.4 us (8%)
  between operations  14 us (5%)
  other arithmetic  11 us (4%)
    reduce_scatter x1, waiting for transfers between devices, body(): lax.psum_scatter(part.reshape(devices, tok_rows, width), BOTH, scatter_di...  116 us
    all_gather x1, waiting for transfers between devices, body(): all_g = lax.all_gather(cotangent[None], BOTH, axis=0, tiled=True)  44.8 us
    all_gather x1, blocking collectives, body(): lax.all_gather(jnp.concatenate([on, weight], axis=1)[None], BOTH, axis=0,...  44 us
    all_gather x1, waiting for transfers between devices, body(): all_x = lax.all_gather(features[None], BOTH, axis=0, tiled=True)  18.8 us
    dot_general x1, matrix products, body(): d_hidden = jnp.dot(rows_g, down_w.T, preferred_element_type=jnp.float32)  6.64 us
  transfers between devices with their start and end apart: 3, of which 3 were waited for; matrix products, arithmetic and copies ran while one was open for 14% of the time, Pallas kernels for 0%

commit v1 on v0

--- a/solution.py
+++ b/solution.py
@@ -20,7 +20,15 @@
     on = jnp.sum(hits.astype(jnp.float32), axis=1)
     weight = jnp.sum(jnp.where(hits, gates[..., None], 0.0), axis=1)
     routes = lax.all_gather(jnp.concatenate([on, weight], axis=1)[None], BOTH, axis=0, tiled=True)
-    all_x = lax.all_gather(features[None], BOTH, axis=0, tiled=True)
+    ways, here = (lax.axis_size(BOTH), lax.axis_index(BOTH))
+    grown, reach = (features[None], 1)
+    while reach < ways:
+        theirs = lax.ppermute(grown, BOTH, [(d, d ^ reach) for d in range(ways)])
+        mine_first = jnp.concatenate([grown, theirs], axis=0)
+        theirs_first = jnp.concatenate([theirs, grown], axis=0)
+        grown = jnp.where(here & reach == 0, mine_first, theirs_first)
+        reach = 2 * reach
+    all_x = grown
     all_g = lax.all_gather(cotangent[None], BOTH, axis=0, tiled=True)
     me = lax.axis_index("local")
     routes = routes.reshape(rows, 2 * experts)

time: 309 us -> 298 us (0.964)
  waiting for transfers between devices: 181 us -> 157 us
  starting transfers between devices: 0.11 us -> 9 us
    all_gather x1, waiting for transfers between devices: 44.8 us -> 0.01 us  [body(): all_g = lax.all_gather(cotangent[None], BOTH, axis=0, tiled=True)]
    ppermute x0 -> x5, waiting for transfers between devices: none -> 43 us  [body(): theirs = lax.ppermute(grown, BOTH, [(d, d ^ reach) for d in range(ways)])]
    all_gather x1 -> x0, waiting for transfers between devices: 18.8 us -> none  [body(): all_x = lax.all_gather(features[None], BOTH, axis=0, tiled=True)]
    ppermute x0 -> x5, starting transfers between devices: none -> 8.92 us  [body(): theirs = lax.ppermute(grown, BOTH, [(d, d ^ reach) for d in range(ways)])]
    select_n x0 -> x3, local copies, waits for them, and re-layouts: none -> 5.44 us  [body(): grown = jnp.where(here & reach == 0, mine_first, theirs_first)]
    unnamed x40 -> x43, local copies, waits for them, and re-layouts: 5.55 us -> 0.98 us
  transfers between devices with their start and end apart: 3 -> 7, of which waited for: 3 -> 5; matrix products, arithmetic and copies ran while one was open for 14% -> 15% of each run, Pallas kernels for 0% -> 0%
where the time goes in v1:
time: 298 us
  waiting for transfers between devices  157 us (53%)
  blocking collectives  43.4 us (15%)
  matrix products  35.5 us (12%)
  local copies, waits for them, and re-layouts  25.4 us (9%)
  between operations  14.3 us (5%)
  other arithmetic  13.1 us (4%)
  starting transfers between devices  9 us (3%)
    reduce_scatter x1, waiting for transfers between devices, body(): lax.psum_scatter(part.reshape(devices, tok_rows, width), BOTH, scatter_di...  114 us
    all_gather x1, blocking collectives, body(): lax.all_gather(jnp.concatenate([on, weight], axis=1)[None], BOTH, axis=0,...  43.4 us
    ppermute x5, waiting for transfers between devices, body(): theirs = lax.ppermute(grown, BOTH, [(d, d ^ reach) for d in range(ways)])  43 us
    ppermute x5, starting transfers between devices, body(): theirs = lax.ppermute(grown, BOTH, [(d, d ^ reach) for d in range(ways)])  8.92 us
    dot_general x1, matrix products, body(): d_hidden = jnp.dot(rows_g, down_w.T, preferred_element_type=jnp.float32)  6.64 us
  transfers between devices with their start and end apart: 7, of which 5 were waited for; matrix products, arithmetic and copies ran while one was open for 15% of the time, Pallas kernels for 0%

profile of v1, /device:TPU:0, one launch (start us, length us, event | category | flops | bytes accessed | tf_op | source)
XLA Modules:
  0.0 297.6 jit_solution(7299173912156811964)
XLA Ops:
  10.0 3.0 %collective-permute-start.1 = (bf16[2,6,7168]{2,1,0:T(8,128)(2,1)S(1)}, bf16[2,6,7168]{2,1,0:T(8,128)(2,1)S(1)}, u32[]{:S(2)}, u32[]{:S(2)}) collective-permute-start(bf16[2,6,7168]{2,1,0:T(8,128)(2,1)S(1)} %maximum_select_fusion.4), channel_id=1, source_target_pairs={{0,2},{1,3},{2,0},{3,1},{4,6},{5,7},{6,4},{7,5},{8,10},{9,11},{10,... | collective-permute-start | bytes 516104 | tf_op jit(solution)/shard_map/ppermute | solution.py:26
  13.0 5.9 %collective-permute-done.1 = bf16[2,6,7168]{2,1,0:T(8,128)(2,1)S(1)} collective-permute-done((bf16[2,6,7168]{2,1,0:T(8,128)(2,1)S(1)}, bf16[2,6,7168]{2,1,0:T(8,128)(2,1)S(1)}, u32[]{:S(2)}, u32[]{:S(2)}) %collective-permute-start.1) | collective-permute-done | bytes 172064 | tf_op jit(solution)/shard_map/ppermute | solution.py:26
  19.1 2.8 collective-permute-start.2
  21.9 20.0 %collective-permute-done.2 = bf16[4,6,7168]{2,1,0:T(8,128)(2,1)S(1)} collective-permute-done((bf16[4,6,7168]{2,1,0:T(8,128)(2,1)S(1)}, bf16[4,6,7168]{2,1,0:T(8,128)(2,1)S(1)}, u32[]{:S(2)}, u32[]{:S(2)}) %collective-permute-start.2) | collective-permute-done | bytes 344096 | tf_op jit(solution)/shard_map/ppermute | solution.py:26
  44.2 15.9 %collective-permute-done.3 = bf16[8,6,7168]{2,0,1:T(8,128)(2,1)S(1)} collective-permute-done((bf16[8,6,7168]{2,0,1:T(8,128)(2,1)S(1)}, bf16[8,6,7168]{2,0,1:T(8,128)(2,1)S(1)}, u32[]{:S(2)}, u32[]{:S(2)}) %collective-permute-start.3) | collective-permute-done | bytes 688160 | tf_op jit(solution)/shard_map/ppermute | solution.py:26
  61.3 1.8 copy.33
  64.7 43.4 %all-gather.2 = f32[32,6,16]{2,1,0:T(8,128)S(1)} all-gather(f32[1,6,16]{2,1,0:T(8,128)S(1)} %maximum_bitcast_fusion), channel_id=2, replica_groups=mesh['group'=4,'local'=8] {'group','local'}, dimensions={0}, use_global_device_ids=true | all-gather | bytes 12672 | tf_op jit(solution)/shard_map/all_gather | solution.py:22
  109.9 3.9 %broadcast_select_fusion = (bf16[32,6,7168]{2,1,0:T(8,128)(2,1)}, bf16[32,6,7168]{2,1,0:T(8,128)(2,1)}) fusion(pred[32,6]{1,0:T(8,128)(4,1)S(1)} %broadcast_in_dim.57, bf16[16,6,7168]{2,1,0:T(8,128)(2,1)S(1)} %maximum_select_fusion.1, bf16[16,6,7168]{2,1,0:T(8,128)(2,1)S(1)} %copy.34, pred[]{:T(512)S(6)} %eq.31), kind=kLoop, calls=%fused_computation.20 | loop fusion | flops 5505024 | bytes 8257729 | tf_op jit(solution)/shard_map/jit(_where)/select_n | solution.py:37
  113.8 4.8 %select_n.98 = bf16[192,7168]{1,0:T(8,128)(2,1)} reshape(bf16[32,6,7168]{2,1,0:T(8,128)(2,1)} %get-tuple-element.6) | data formatting | bytes 5505024 | tf_op jit(solution)/shard_map/jit(_where)/select_n | solution.py:37
  118.6 5.6 %fusion.6 = f32[192,512]{1,0:T(8,128)S(1)} fusion(bf16[192,7168]{1,0:T(8,128)(2,1)} %select_n.98, bf16[1,7168,512]{2,1,0:T(8,128)(2,1)} %param.11), kind=kOutput, calls=%fused_computation.10 | convolution fusion | flops 1409286144 | bytes 10485760 | tf_op jit(solution)/shard_map/dot_general | solution.py:42
  124.5 2.4 fusion.9
  126.9 4.8 %multiply_convert_fusion = bf16[32,6,7168]{2,1,0:T(8,128)(2,1)} fusion(f32[32,6]{1,0:T(8,128)S(1)} %mul.41, bf16[32,6,7168]{2,1,0:T(8,128)(2,1)} %all-gather.6.cloned.1.call-done), kind=kLoop, calls=%fused_computation.17 | loop fusion | flops 4128768 | bytes 5505792 | tf_op jit(solution)/shard_map/convert_element_type | solution.py:38
  131.7 4.8 %convert_element_type.50 = bf16[192,7168]{1,0:T(8,128)(2,1)} reshape(bf16[32,6,7168]{2,1,0:T(8,128)(2,1)} %multiply_convert_fusion) | data formatting | bytes 5505024 | tf_op jit(solution)/shard_map/convert_element_type | solution.py:38
  136.5 6.6 %multiply_convert_fusion.4 = (bf16[192,512]{1,0:T(8,128)(2,1)S(1)}, bf16[192,512]{1,0:T(8,128)(2,1)S(1)}) fusion(f32[192,512]{1,0:T(8,128)S(1)} %fusion.6, f32[192,512]{1,0:T(8,128)} %fusion.9, bf16[192,7168]{1,0:T(8,128)(2,1)} %convert_element_type.50, bf16[1,512,7168]{2,1,0:T(8,128)(2,1)} %param.13), kind=kOutput, calls=%fused_computation.27 | convolution fusion | flops 1410564096 | bytes 11272192 | tf_op jit(solution)/shard_map/dot_general | solution.py:46
  143.2 2.5 fusion.4
  145.8 2.5 fusion.3
  148.3 2.7 reshape.93
  151.0 3.2 %select_n.99 = bf16[192,7168]{1,0:T(8,128)(2,1)S(1)} reshape(bf16[32,6,7168]{2,1,0:T(8,128)(2,1)} %get-tuple-element.7) | data formatting | bytes 5505024 | tf_op jit(solution)/shard_map/jit(_where)/select_n | solution.py:29
  154.3 5.2 %reshape.108 = f32[192,7168]{1,0:T(8,128)} reshape(bf16[32,6,7168]{2,1,0:T(8,128)(2,1)} %all-gather.6.cloned.1.call-done) | data formatting | bytes 8257536 | tf_op jit(solution)/shard_map/convert_element_type | solution.py:38
  159.5 5.3 %fusion.1 = bf16[1,7168,512]{2,1,0:T(8,128)(2,1)} fusion(bf16[192,512]{1,0:T(8,128)(2,1)S(1)} %copy-done.3, bf16[192,7168]{1,0:T(8,128)(2,1)S(1)} %select_n.99, pred[192]{0:T(512)(128)(4,1)S(1)} %copy-done.9), kind=kOutput, calls=%fused_computation.4 | convolution fusion | flops 1414332416 | bytes 10289344 | tf_op jit(solution)/shard_map/dot_general | solution.py:57
  164.8 5.3 %fusion = bf16[1,7168,512]{2,1,0:T(8,128)(2,1)} fusion(bf16[192,512]{1,0:T(8,128)(2,1)S(1)} %copy-done.5, bf16[192,7168]{1,0:T(8,128)(2,1)S(1)} %select_n.99, pred[192]{0:T(512)(128)(4,1)S(1)} %copy-done.9), kind=kOutput, calls=%fused_computation.3 | convolution fusion | flops 1414332416 | bytes 10289344 | tf_op jit(solution)/shard_map/dot_general | solution.py:56
  170.2 5.2 %fusion.2 = bf16[1,512,7168]{2,1,0:T(8,128)(2,1)} fusion(f32[192,7168]{1,0:T(8,128)S(1)} %bitcast.36, f32[192]{0:T(256)S(1)} %copy-done.7, f32[192,512]{1,0:T(8,128)S(1)} %copy-done.1, f32[192,512]{1,0:T(8,128)S(1)} %fusion.6), kind=kOutput, calls=%fused_computation.5 | convolution fusion | flops 1416298496 | bytes 13632256 | tf_op jit(solution)/shard_map/dot_general | solution.py:55
  175.4 113.8 %reduce-scatter.2.cloned.1.call-done = bf16[1,6,7168]{2,1,0:T(8,128)(2,1)} async-done(((bf16[32,6,7168]{2,1,0:T(8,128)(2,1)}), bf16[1,6,7168]{2,1,0:T(8,128)(2,1)}) %reduce-scatter.2.cloned.1.call-update) | async-done | bytes 86032 | tf_op jit(solution)/shard_map/reduce_scatter | solution.py:52
  289.2 1.6 bitcast_convert_fusion
  (70 shorter events, 10.1 us)
Async XLA Ops:
  7.2 119.8 %all-gather.6.cloned.1.call-start = ((), (), s32[]{:S(2)}) async-start(), calls=%async_computation.2 | async-start | bytes 3784704 | tf_op jit(solution)/shard_map/all_gather | solution.py:32
  7.2 1.7 collective-permute-start
  10.0 8.9 %collective-permute-start.1 = (bf16[2,6,7168]{2,1,0:T(8,128)(2,1)S(1)}, bf16[2,6,7168]{2,1,0:T(8,128)(2,1)S(1)}, u32[]{:S(2)}, u32[]{:S(2)}) collective-permute-start(bf16[2,6,7168]{2,1,0:T(8,128)(2,1)S(1)} %maximum_select_fusion.4), channel_id=1, source_target_pairs={{0,2},{1,3},{2,0},{3,1},{4,6},{5,7},{6,4},{7,5},{8,10},{9,11},{10,... | collective-permute-start | bytes 516104 | tf_op jit(solution)/shard_map/ppermute | solution.py:26
  19.1 22.9 %collective-permute-start.2 = (bf16[4,6,7168]{2,1,0:T(8,128)(2,1)S(1)}, bf16[4,6,7168]{2,1,0:T(8,128)(2,1)S(1)}, u32[]{:S(2)}, u32[]{:S(2)}) collective-permute-start(bf16[4,6,7168]{2,1,0:T(8,128)(2,1)S(1)} %maximum_select_fusion.3), channel_id=1, source_target_pairs={{0,4},{1,5},{2,6},{3,7},{4,0},{5,1},{6,2},{7,3},{8,12},{9,13},{10,... | collective-permute-start | bytes 1032200 | tf_op jit(solution)/shard_map/ppermute | solution.py:26
  42.7 17.4 %collective-permute-start.3 = (bf16[8,6,7168]{2,0,1:T(8,128)(2,1)S(1)}, bf16[8,6,7168]{2,0,1:T(8,128)(2,1)S(1)}, u32[]{:S(2)}, u32[]{:S(2)}) collective-permute-start(bf16[8,6,7168]{2,0,1:T(8,128)(2,1)S(1)} %copy.30), channel_id=1, source_target_pairs={{0,8},{1,9},{2,10},{3,11},{4,12},{5,13},{6,14},{7,15},{8,0},{9,1},... | collective-permute-start | bytes 2064392 | tf_op jit(solution)/shard_map/ppermute | solution.py:26
  44.1 245.0 %reduce-scatter.2.cloned.1.call-start = ((), (), s32[]{:S(2)}) async-start(), calls=%async_computation.1 | async-start | bytes 3784704 | tf_op jit(solution)/shard_map/reduce_scatter | solution.py:52
  60.5 3.8 %copy-start.10 = (s32[6,4]{0,1:T(4,128)S(1)}, s32[6,4]{0,1:T(4,128)}, u32[]{:S(2)}) copy-start(s32[6,4]{0,1:T(4,128)} %param.9) | copy-start | bytes 292
  60.5 3.9 %copy-start.11 = (f32[6,4]{0,1:T(4,128)S(1)}, f32[6,4]{0,1:T(4,128)}, u32[]{:S(2)}) copy-start(f32[6,4]{0,1:T(4,128)} %param.10) | copy-start | bytes 292
  63.1 46.0 %collective-permute-start.4 = (bf16[16,6,7168]{2,0,1:T(8,128)(2,1)}, bf16[16,6,7168]{2,0,1:T(8,128)(2,1)S(1)}, u32[]{:S(2)}, u32[]{:S(2)}) collective-permute-start(bf16[16,6,7168]{2,0,1:T(8,128)(2,1)} %copy.33), channel_id=1, source_target_pairs={{0,16},{1,17},{2,18},{3,19},{4,20},{5,21},{6,22},{7,23},{8,24},{9,... | collective-permute-start | bytes 4128776 | tf_op jit(solution)/shard_map/ppermute | solution.py:26
  108.9 4.8 %copy-start.6 = (f32[192]{0:T(256)}, f32[192]{0:T(256)S(1)}, u32[]{:S(2)}) copy-start(f32[192]{0:T(256)S(1)} %dynamic-slice_reduce_fusion) | copy-start | bytes 2308
  113.8 10.4 %slice-start.4 = ((s8[7340032]{0:T(1024)(128)(4,1)}), s8[3145728]{0:T(1024)(128)(4,1)S(1)}, s32[]{:S(2)}) async-start(s8[7340032]{0:T(1024)(128)(4,1)} %bitcast.39), calls=%async_computation.7 | async-start | bytes 6291456
  118.6 5.7 %slice-start.5 = ((s8[7340032]{0:T(1024)(128)(4,1)}), s8[4194304]{0:T(1024)(128)(4,1)S(1)}, s32[]{:S(2)}) async-start(s8[7340032]{0:T(1024)(128)(4,1)} %bitcast.39), calls=%async_computation.8 | async-start | bytes 8388608
  118.6 6.0 %copy-start = (bf16[192,7168]{1,0:T(8,128)(2,1)S(1)}, bf16[192,7168]{1,0:T(8,128)(2,1)}, u32[]{:S(2)}) copy-start(bf16[192,7168]{1,0:T(8,128)(2,1)} %select_n.98) | copy-start | bytes 8257540
  131.7 11.5 %slice-start.2 = ((s8[7340032]{0:T(1024)(128)(4,1)}), s8[3145728]{0:T(1024)(128)(4,1)S(1)}, s32[]{:S(2)}) async-start(s8[7340032]{0:T(1024)(128)(4,1)} %bitcast.37), calls=%async_computation.5 | async-start | bytes 6291456
  136.5 6.7 %slice-start.3 = ((s8[7340032]{0:T(1024)(128)(4,1)}), s8[4194304]{0:T(1024)(128)(4,1)S(1)}, s32[]{:S(2)}) async-start(s8[7340032]{0:T(1024)(128)(4,1)} %bitcast.37), calls=%async_computation.6 | async-start | bytes 8388608
  136.5 9.3 %slice-start.6 = ((s8[7340032]{0:T(1024)(128)(4,1)}), s8[4194304]{0:T(1024)(128)(4,1)S(1)}, s32[]{:S(2)}) async-start(s8[7340032]{0:T(1024)(128)(4,1)} %bitcast.41), calls=%async_computation.9 | async-start | bytes 8388608
  143.1 2.6 copy-start.4
  154.3 5.2 %copy-start.3 = (bf16[192,512]{1,0:T(8,128)(2,1)S(1)}, bf16[192,512]{1,0:T(8,128)(2,1)}, u32[]{:S(2)}) copy-start(bf16[192,512]{1,0:T(8,128)(2,1)} %copy-done.2) | copy-start | bytes 589828
  154.3 5.2 %copy-start.9 = (pred[192]{0:T(512)(128)(4,1)S(1)}, pred[192]{0:T(512)(128)(4,1)}, u32[]{:S(2)}) copy-start(pred[192]{0:T(512)(128)(4,1)} %copy-done.8) | copy-start | bytes 580
  159.5 5.3 %copy-start.5 = (bf16[192,512]{1,0:T(8,128)(2,1)S(1)}, bf16[192,512]{1,0:T(8,128)(2,1)}, u32[]{:S(2)}) copy-start(bf16[192,512]{1,0:T(8,128)(2,1)} %copy-done.4) | copy-start | bytes 589828
  159.5 10.6 %slice-start = ((s8[5505024]{0:T(1024)(128)(4,1)}), s8[4194304]{0:T(1024)(128)(4,1)S(1)}, s32[]{:S(2)}) async-start(s8[5505024]{0:T(1024)(128)(4,1)} %bitcast.35), calls=%async_computation.3 | async-start | bytes 8388608
  164.8 5.3 %slice-start.1 = ((s8[5505024]{0:T(1024)(128)(4,1)}), s8[1310720]{0:T(1024)(128)(4,1)S(1)}, s32[]{:S(2)}) async-start(s8[5505024]{0:T(1024)(128)(4,1)} %bitcast.35), calls=%async_computation.4 | async-start | bytes 2621440
  164.8 5.3 %copy-start.1 = (f32[192,512]{1,0:T(8,128)S(1)}, f32[192,512]{1,0:T(8,128)}, u32[]{:S(2)}) copy-start(f32[192,512]{1,0:T(8,128)} %fusion.9) | copy-start | bytes 1179652
  164.8 5.3 %copy-start.7 = (f32[192]{0:T(256)S(1)}, f32[192]{0:T(256)}, u32[]{:S(2)}) copy-start(f32[192]{0:T(256)} %copy-done.6) | copy-start | bytes 2308
  (3 other events, 5.7 us)
Sparse Core Ops, SparseCore 0:
  44.3 66.1 all-gather.5
  151.1 137.9 reduce-scatter.1
